TPU v7x, 128 devices: a whole 4x4x4 slice. The times are simulated.
128 devices in a mesh: tm: 16 (over z, y), space: 8 (over x, core).
Axes of the slice: x: 4, y: 4, z: 4, core: 2. Of those that a mesh axis runs over, the one named last changes fastest.
Arguments:
- state: float32 [2048, 8192], P('tm', 'space'), may hold values from -4 to 4
- space_factor: bfloat16 [8192, 8192], P('space'), as said below
- time_factor: float32 [2048, 2048], replicated, as said below
- footprints: bfloat16 [1024, 8, 128, 256], P('tm', 'space'), may hold values from -0.125 to 0.125
- tile_obs: int32 [1024, 8], P('tm', 'space'), may hold values from 0 to 1023, as said below
- tile_block: int32 [1024, 8], P('tm', 'space'), may hold values from 0 to 31, as said below
- tile_time: int32 [1024, 8], P('tm', 'space'), may hold values from 0 to 2047
- tile_count: int32 [16, 8], P('tm', 'space'), may hold values from 8 to 64, as said below
- obs_dep: float32 [1024, 128], P('tm'), may hold values from -6 to 6
- obs_weight: float32 [1024, 128], P('tm'), may hold values from 0.25 to 4
Outputs:
- gradient: float32 [2048, 8192], P('tm', 'space')
Inputs may be any that keep to these rules, and one draw needn't show every extreme that they name: `tile_obs`: the observation tile of a slot on tm index i lies among that index's own tiles, i * 64 to (i + 1) * 64 - 1. `tile_block`: the cell block of a slot on space index j lies in that index's cells, j * 4 to (j + 1) * 4 - 1. `tile_count`: some device has all 64 slots live. `space_factor`: the identity plus off-diagonal entries of half the identity's row weight. `time_factor`: the identity plus off-diagonal entries of half the identity's row weight.
All inputs are finite; a program needn't handle non-finite values.
Results may differ from a plain program's by a relative error of at most 0.0065.
Values may be sent and summed in bfloat16 or wider, within the bound.
A program may use at most 128 MiB of HBM per device.

v0:
```python
import jax
import jax.numpy as jnp
from jax import lax
from jax.sharding import PartitionSpec as P


def local(
    state,
    space_factor,
    time_factor,
    footprints,
    tile_obs,
    tile_block,
    tile_time,
    tile_count,
    obs_dep,
    obs_weight,
):
    highest = lax.Precision.HIGHEST
    time_rows, cell_cols = state.shape
    all_times = time_factor.shape[0]
    cap_slots = footprints.shape[0]
    obs_rows = footprints.shape[2]
    block_cells = footprints.shape[3]
    local_blocks = cell_cols // block_cells
    owned_tiles = obs_dep.shape[0]
    state_low = state.astype(jnp.bfloat16)
    factor_cols = space_factor
    spread = lax.dot_general(
        lax.all_gather(state_low, "space", axis=1, tiled=True),
        factor_cols,
        (((1,), (1,)), ((), ())),
        preferred_element_type=jnp.float32,
    )
    tile_maps = footprints.reshape(cap_slots, obs_rows, block_cells)
    obs_local = tile_obs[:, 0] - lax.axis_index("tm") * owned_tiles
    block_local = tile_block[:, 0] - lax.axis_index("space") * local_blocks
    time_at = tile_time[:, 0]
    live_mask = (jnp.arange(cap_slots, dtype=jnp.int32) < tile_count[0, 0]).astype(jnp.float32)
    factor_cols = time_factor
    flux = jnp.zeros((all_times, cell_cols), jnp.float32) + jnp.dot(
        factor_cols,
        lax.all_gather(spread.astype(jnp.bfloat16), "tm", axis=0, tiled=True).astype(jnp.float32),
        precision=highest,
    )
    flux_cols = flux.astype(jnp.bfloat16).reshape(all_times, local_blocks, block_cells)[
        time_at, block_local
    ]
    tile_sims = (
        jnp.einsum("kob,kb->ko", tile_maps, flux_cols, preferred_element_type=jnp.float32)
        * live_mask[:, None]
    )
    obs_select = (obs_local[:, None] == jnp.arange(owned_tiles, dtype=jnp.int32)[None, :]).astype(
        jnp.float32
    )
    sim_part = lax.dot_general(obs_select, tile_sims, (((0,), (0,)), ((), ())), precision=highest)
    evolved = lax.psum(sim_part.astype(jnp.bfloat16), "space").astype(jnp.float32)
    depart_low = (obs_weight * (evolved - obs_dep)).astype(jnp.bfloat16)
    tile_depart = depart_low[obs_local]
    tile_back = (
        jnp.einsum("kob,ko->kb", tile_maps, tile_depart, preferred_element_type=jnp.float32)
        * live_mask[:, None]
    )
    q_part = (
        jnp.zeros((all_times, local_blocks, block_cells), jnp.float32)
        .at[time_at, block_local]
        .add(tile_back)
    )
    q_part = q_part.reshape(all_times, cell_cols)
    factor_cols = time_factor
    adjoint = lax.psum_scatter(
        lax.dot_general(factor_cols, q_part, (((0,), (0,)), ((), ())), precision=highest),
        "tm",
        scatter_dimension=0,
        tiled=True,
    )
    adjoint_low = adjoint.astype(jnp.bfloat16)
    cell_terms = jnp.dot(adjoint_low, space_factor, preferred_element_type=jnp.float32)
    prior_back = lax.psum_scatter(
        cell_terms.astype(jnp.bfloat16), "space", scatter_dimension=1, tiled=True
    ).astype(jnp.float32)
    return state + prior_back


def solution(mesh):
    return jax.shard_map(
        local,
        mesh=mesh,
        in_specs=(
            P("tm", "space"),
            P("space", None),
            P(),
            P("tm", "space", None, None),
            P("tm", "space"),
            P("tm", "space"),
            P("tm", "space"),
            P("tm", "space"),
            P("tm", None),
            P("tm", None),
        ),
        out_specs=P("tm", "space"),
        check_vma=False,
    )
```

profile of v0, /device:TPU:0, one launch (start us, length us, event | category | flops | bytes accessed | tf_op | source)
XLA Modules:
  0.0 387.3 jit_solution(15894813467778132030)
XLA Ops:
  6.5 0.0 all-gather.3.cloned.1.call-start
  6.5 1.8 convert_element_type.39
  8.3 0.0 all-gather.3.cloned.1.call-update
  8.3 0.0 copy-start.5
  8.4 0.0 copy-start.3
  8.4 0.0 copy-start.4
  8.4 0.0 all-gather.5.cloned.1.call-start
  8.4 28.3 %all-gather.3.cloned.1.call-done = bf16[128,8192]{1,0:T(8,128)(2,1)} async-done(((bf16[128,1024]{1,0:T(8,128)(2,1)}), bf16[128,8192]{1,0:T(8,128)(2,1)}) %all-gather.3.cloned.1.call-update) | async-done | bytes 2097168 | tf_op jit(solution)/shard_map/all_gather | solution.py:30
  36.7 12.8 %convolution_convert_fusion.2 = bf16[128,1024]{1,0:T(8,128)(2,1)} fusion(bf16[128,8192]{1,0:T(8,128)(2,1)} %all-gather.3.cloned.1.call-done, bf16[1024,8192]{1,0:T(8,128)(2,1)} %param.11), kind=kOutput, calls=%fused_computation.10 | convolution fusion | flops 2147614720 | bytes 19136512 | tf_op jit(solution)/shard_map/dot_general | solution.py:29
  49.5 0.0 all-gather.5.cloned.1.call-update
  49.5 0.2 reduce-scatter.3.cloned.1.call-start
  50.4 0.0 copy-done.5
  50.4 0.0 copy-done.3
  50.4 0.0 copy-done.4
  50.5 51.2 %all-gather.5.cloned.1.call-done = bf16[2048,1024]{1,0:T(8,128)(2,1)} async-done(((bf16[128,1024]{1,0:T(8,128)(2,1)}), bf16[2048,1024]{1,0:T(8,128)(2,1)}) %all-gather.5.cloned.1.call-update) | async-done | bytes 4194320 | tf_op jit(solution)/shard_map/all_gather | solution.py:43
  101.6 36.3 %convolution_convert_fusion.1 = bf16[1024,2048]{1,0:T(8,128)(2,1)} fusion(bf16[2048,1024]{1,0:T(8,128)(2,1)} %all-gather.5.cloned.1.call-done, f32[2048,2048]{1,0:T(8,128)} %param.12), kind=kOutput, calls=%fused_computation.9 | convolution fusion | flops 51541704704 | bytes 25165824 | tf_op jit(solution)/shard_map/dot_general | solution.py:41
  137.9 0.0 copy-start.1
  137.9 0.0 copy-start.2
  137.9 7.5 %copy.11 = bf16[2048,4,256]{2,1,0:T(4,128)(2,1)} copy(bf16[2048,4,256]{0,2,1:T(8,128)(2,1)} %bitcast.36) | data formatting | bytes 8388608 | tf_op jit(solution)/shard_map/reshape | solution.py:46
  145.3 1.6 gather_fusion
  146.9 3.4 fusion.2
  150.3 0.3 convolution_convert_fusion.3
  150.6 25.6 %psum.7 = bf16[64,128]{1,0:T(8,128)(2,1)S(1)} all-reduce(bf16[64,128]{1,0:T(8,128)(2,1)S(1)} %convolution_convert_fusion.3), channel_id=1, replica_groups=mesh['tm'=16,'space'=8] {'space'}, use_global_device_ids=true, to_apply=%region_0.0 | all-reduce | flops 8192 | bytes 32768 | tf_op jit(solution)/shard_map/psum | solution.py:57
  176.2 0.0 copy-done.1
  176.2 0.0 copy-done.2
  176.2 0.6 gather_fusion.1
  176.8 2.8 fusion
  179.7 0.1 bitcast_multiply_fusion
  179.7 3.9 %broadcast_in_dim.2 = f32[2048,4,256]{2,1,0:T(4,128)} broadcast(f32[]{:T(128)} %constant.8.clone.1), dimensions={} | broadcast | bytes 8388612 | tf_op jit(solution)/shard_map/broadcast_in_dim | solution.py:65
  183.6 7.4 %scatter_fusion = f32[2048,4,256]{2,1,0:T(4,128)} fusion(f32[2048,4,256]{2,1,0:T(4,128)} %broadcast_in_dim.2, s32[64]{0:T(128)S(1)} %get-tuple-element.5, f32[64,256]{1,0:T(8,128)S(1)} %bitcast_multiply_fusion), kind=kCustom, calls=%fused_computation.2 | custom fusion | flops 16384 | bytes 197120 | tf_op jit(solution)/shard_map/scatter-add | solution.py:67
  191.0 5.5 %copy.16 = f32[256,8,4,256]{3,1,2,0:T(8,128)S(1)} copy(f32[256,8,4,256]{3,2,1,0:T(4,128)} %bitcast.34) | data formatting | bytes 16777216
  196.5 57.1 %convolution_bitcast_fusion = f32[2048,1024]{0,1:T(8,128)} fusion(f32[2048,1024]{1,0:T(8,128)S(1)} %bitcast.35, f32[2048,2048]{1,0:T(8,128)} %param.12), kind=kOutput, calls=%fused_computation.4 | convolution fusion | flops 51539607552 | bytes 33554432 | tf_op jit(solution)/shard_map/dot_general | solution.py:72
  253.6 0.0 reduce-scatter.3.cloned.1.call-update
  253.6 0.0 copy-start
  253.6 0.0 reduce-scatter.5.cloned.1.call-start
  253.7 82.6 %reduce-scatter.3.cloned.1.call-done = f32[128,1024]{0,1:T(8,128)} async-done(((f32[2048,1024]{0,1:T(8,128)}), f32[128,1024]{0,1:T(8,128)}) %reduce-scatter.3.cloned.1.call-update) | async-done | bytes 524304 | tf_op jit(solution)/shard_map/reduce_scatter | solution.py:71
  336.3 9.8 %convolution_convert_fusion = bf16[128,8192]{1,0:T(8,128)(2,1)} fusion(bf16[1024,8192]{1,0:T(8,128)(2,1)} %param.11, f32[128,1024]{0,1:T(8,128)} %reduce-scatter.3.cloned.1.call-done), kind=kOutput, calls=%fused_computation.3 | convolution fusion | flops 2148663296 | bytes 19398656 | tf_op jit(solution)/shard_map/dot_general | solution.py:78
  346.0 0.0 reduce-scatter.5.cloned.1.call-update
  346.1 32.9 %reduce-scatter.5.cloned.1.call-done = bf16[128,1024]{1,0:T(8,128)(2,1)} async-done(((bf16[128,8192]{1,0:T(8,128)(2,1)}), bf16[128,1024]{1,0:T(8,128)(2,1)}) %reduce-scatter.5.cloned.1.call-update) | async-done | bytes 262160 | tf_op jit(solution)/shard_map/reduce_scatter | solution.py:79
  378.9 0.0 copy-done
  378.9 1.8 convert_add_fusion
  (5 shorter events, 0.0 us)
Async XLA Ops:
  6.5 30.1 %all-gather.3.cloned.1.call-start = ((), (), s32[]{:S(2)}) async-start(), calls=%async_computation.2 | async-start | bytes 2359296 | tf_op jit(solution)/shard_map/all_gather | solution.py:30
  8.3 42.0 %copy-start.5 = (s32[64,1]{0,1:T(1,128)S(1)}, s32[64,1]{0,1:T(1,128)}, u32[]{:S(2)}) copy-start(s32[64,1]{0,1:T(1,128)} %param.14) | copy-start | bytes 772
  8.4 42.1 %copy-start.3 = (s32[64,1]{0,1:T(1,128)S(1)}, s32[64,1]{0,1:T(1,128)}, u32[]{:S(2)}) copy-start(s32[64,1]{0,1:T(1,128)} %param.16) | copy-start | bytes 772
  8.4 42.1 %copy-start.4 = (s32[64,1]{0,1:T(1,128)S(1)}, s32[64,1]{0,1:T(1,128)}, u32[]{:S(2)}) copy-start(s32[64,1]{0,1:T(1,128)} %param.15) | copy-start | bytes 772
  8.4 93.2 %all-gather.5.cloned.1.call-start = ((), (), s32[]{:S(2)}) async-start(), calls=%async_computation.3 | async-start | bytes 4456448 | tf_op jit(solution)/shard_map/all_gather | solution.py:43
  49.5 286.8 %reduce-scatter.3.cloned.1.call-start = ((), (), s32[]{:S(2)}) async-start(), calls=%async_computation.4 | async-start | bytes 8912896 | tf_op jit(solution)/shard_map/reduce_scatter | solution.py:71
  137.9 38.3 %copy-start.1 = (f32[64,128]{1,0:T(8,128)S(1)}, f32[64,128]{1,0:T(8,128)}, u32[]{:S(2)}) copy-start(f32[64,128]{1,0:T(8,128)} %param.19) | copy-start | bytes 98308
  137.9 38.3 %copy-start.2 = (f32[64,128]{1,0:T(8,128)S(1)}, f32[64,128]{1,0:T(8,128)}, u32[]{:S(2)}) copy-start(f32[64,128]{1,0:T(8,128)} %param.18) | copy-start | bytes 98308
  253.6 125.3 %copy-start = (f32[128,1024]{1,0:T(8,128)S(1)}, f32[128,1024]{1,0:T(8,128)}, u32[]{:S(2)}) copy-start(f32[128,1024]{1,0:T(8,128)} %param.10) | copy-start | bytes 1572868
  253.6 125.3 %reduce-scatter.5.cloned.1.call-start = ((), (), s32[]{:S(2)}) async-start(), calls=%async_computation.5 | async-start | bytes 2359296 | tf_op jit(solution)/shard_map/reduce_scatter | solution.py:79
Sparse Core Ops, SparseCore 0:
  9.0 27.5 all-gather.2
  49.6 51.9 all-gather.4
  253.7 82.4 reduce-scatter.2
  346.2 32.7 reduce-scatter.4
where the time goes:
time: 388 us; the launch traced here: 387 us
  waiting for transfers between devices  195 us (50%)
  matrix products  122 us (31%)
  blocking collectives  25.6 us (7%)
  local copies, waits for them, and re-layouts  19 us (5%)
  between operations  13.9 us (4%)
  other arithmetic  11.1 us (3%)
    reduce_scatter x1, waiting for transfers between devices, local(): lax.psum_scatter(lax.dot_general(factor_cols, q_part, (((0,), (0,)), ((),...  82.6 us
    dot_general x1, matrix products, local(): lax.dot_general(factor_cols, q_part, (((0,), (0,)), ((), ())), precision=...  57.1 us
    all_gather x1, waiting for transfers between devices, local(): lax.all_gather(spread.astype(jnp.bfloat16), 'tm', axis=0, tiled=True)  51.2 us
    dot_general x1, matrix products, local(): jnp.dot(factor_cols, lax.all_gather(spread.astype(jnp.bfloat16), 'tm', ax...  36.3 us
    reduce_scatter x1, waiting for transfers between devices, local(): lax.psum_scatter(cell_terms.astype(jnp.bfloat16), 'space', scatter_dimens...  32.9 us
    all_gather x1, waiting for transfers between devices, local(): lax.all_gather(state_low, 'space', axis=1, tiled=True)  28.3 us
    psum x1, blocking collectives, local(): lax.psum(sim_part.astype(jnp.bfloat16), 'space').astype(jnp.float32)  25.6 us
    dot_general x1, matrix products, local(): lax.dot_general(lax.all_gather(state_low, 'space', axis=1, tiled=True), f...  12.8 us
  transfers between devices with their start and end apart: 4, of which 4 were waited for; matrix products, arithmetic and copies ran while one was open for 0% of the time, Pallas kernels for 0%

commit v1 on v0

v1 whole, which is shorter than its diff:
```python
import functools

import jax
import jax.numpy as jnp
from jax import lax
from jax.experimental import pallas as pl
from jax.experimental.pallas import tpu as pltpu
from jax.sharding import PartitionSpec as P

MESH = pl.DeviceIdType.MESH
F32 = jnp.float32
BF16 = jnp.bfloat16
NX = 4
NTM = 16
NSP = 8
SLOTS = 64
ROWS = 128
HALF = ROWS // 2
COLS = 1024
BLK = 256
NBLK = COLS // BLK
OBS = 128
TIMES = 2048
OWN, RIGHT, OPP, LEFT = 0, 1, 2, 3


def nt_dot(a, b):
    return lax.dot_general(a, b, (((1,), (1,)), ((), ())), preferred_element_type=F32)


def nn_dot(a, b):
    return jnp.dot(a, b, preferred_element_type=F32)


def kernel(
    state_hbm,
    space_hbm,
    time_hbm,
    foot_hbm,
    obs_hbm,
    block_hbm,
    when_hbm,
    count_hbm,
    dep_hbm,
    weight_hbm,
    out_hbm,
    state_v,
    space_v,
    time_v,
    foot_v,
    obs_v,
    block_v,
    when_v,
    count_v,
    dep_v,
    weight_v,
    out_v,
    xall,
    spread_v,
    time_t,
    meta_out,
    meta_in,
    gt4,
    g4,
    part_out,
    part_in,
    sims_v,
    evo_out,
    evo_in,
    back_out,
    back_in,
    adj_v,
    sib_out,
    sib_in,
    term_v,
    hop_out,
    hop_in,
    lsem,
    ssem,
    rsem,
):
    tm = lax.axis_index("tm")
    sp = lax.axis_index("space")
    z, y = lax.div(tm, NX), lax.rem(tm, NX)
    x, core = lax.div(sp, 2), lax.rem(sp, 2)
    other = 1 - core

    def at_x(rel, c):
        return lax.rem(x + rel, NX) * 2 + c

    def plus(e):
        dz, dy = divmod(e, NX)
        return lax.rem(z + dz, NX) * NX + lax.rem(y + dy, NX)

    def minus(e):
        dz, dy = divmod(e, NX)
        return lax.rem(z + NX - dz, NX) * NX + lax.rem(y + NX - dy, NX)

    loads = []

    def load(src, dst):
        copy = pltpu.make_async_copy(src, dst, lsem.at[len(loads)])
        copy.start()
        loads.append(copy)
        return copy

    sends = []

    def send(src, dst, **where):
        n = len(sends)
        copy = pltpu.make_async_remote_copy(
            src_ref=src,
            dst_ref=dst,
            send_sem=ssem.at[n],
            recv_sem=rsem.at[n],
            device_id=where,
            device_id_type=MESH,
        )
        copy.start()
        sends.append(copy)
        return copy

    ld_state = load(state_hbm, state_v)
    ld_when = load(when_hbm, when_v)
    ld_block = load(block_hbm, block_v)
    ld_count = load(count_hbm, count_v)
    ld_obs = load(obs_hbm, obs_v)

    def load_space(rel, c):
        cols = pl.ds(pl.multiple_of(at_x(rel, c) * COLS, COLS), COLS)
        return load(space_hbm.at[:, cols], space_v.at[rel, 0 if c is core else 1])

    ld_space = {}
    ld_space[OWN, 0] = load_space(OWN, core)
    ld_time = load(time_hbm.at[:, pl.ds(pl.multiple_of(tm * ROWS, ROWS), ROWS)], time_v)
    for rel in (OWN, RIGHT, LEFT, OPP):
        for c in (0, 1):
            if (rel, c) != (OWN, 0):
                ld_space[rel, c] = load_space(rel, other if c else core)
    ld_foot = load(foot_hbm, foot_v)
    ld_dep = load(dep_hbm, dep_v)
    ld_weight = load(weight_hbm, weight_v)

    barrier = pltpu.get_barrier_semaphore()
    for e in range(1, NTM):
        pl.semaphore_signal(barrier, inc=1, device_id={"tm": plus(e)}, device_id_type=MESH)
    for d in range(1, NSP):
        pl.semaphore_signal(
            barrier, inc=1, device_id={"space": lax.rem(sp + d, NSP)}, device_id_type=MESH
        )
    ld_state.wait()
    xall[OWN, 0] = state_v[...].astype(BF16)
    ld_when.wait()
    ld_block.wait()
    ld_count.wait()
    lane = lax.broadcasted_iota(jnp.int32, (1, SLOTS), 1)
    code = when_v[...] * 8 + (block_v[...] - sp * NBLK)
    code = jnp.where(lane < count_v[...], code, -8)
    zero = jnp.zeros((1, SLOTS), jnp.int32)
    meta_out[0] = jnp.broadcast_to(jnp.concatenate([code, zero], axis=1), (8, 2 * SLOTS))
    meta_out[1] = jnp.broadcast_to(jnp.concatenate([zero, code], axis=1), (8, 2 * SLOTS))
    meta_in[0] = meta_out[0]
    pl.semaphore_wait(barrier, NTM - 1 + NSP - 1)

    right, left = at_x(RIGHT, core), at_x(LEFT, core)
    sibling = at_x(OWN, other)
    top, low = pl.ds(0, HALF), pl.ds(HALF, HALF)

    from_left0 = send(xall.at[OWN, 0, top], xall.at[LEFT, 0, top], space=right)
    from_right1 = send(xall.at[OWN, 0, low], xall.at[RIGHT, 0, low], space=left)
    from_left1 = send(xall.at[OWN, 0, low], xall.at[LEFT, 0, low], space=right)
    from_right0 = send(xall.at[OWN, 0, top], xall.at[RIGHT, 0, top], space=left)
    from_sib = {OWN: [send(xall.at[OWN, 0], xall.at[OWN, 1], space=sibling)]}
    from_meta = [None] + [
        send(meta_out.at[e % 2], meta_in.at[e], tm=plus(e)) for e in range(1, NTM)
    ]

    def add_spread(rel, c, first=False):
        ld_space[rel, c].wait()

        @pl.loop(0, COLS // BLK)
        def _(n):
            cols = pl.ds(pl.multiple_of(n * BLK, BLK), BLK)
            term = nt_dot(xall[rel, c], space_v[rel, c, cols, :])
            if first:
                spread_v[:, cols] = term
            else:
                spread_v[:, cols] += term

    add_spread(OWN, 0, first=True)
    from_left0.wait_recv()
    from_opp0 = send(xall.at[LEFT, 0, top], xall.at[OPP, 0, top], space=right)
    from_right1.wait_recv()
    from_opp1 = send(xall.at[RIGHT, 0, low], xall.at[OPP, 0, low], space=left)
    from_sib[LEFT] = [send(xall.at[LEFT, 0, top], xall.at[LEFT, 1, top], space=sibling)]
    from_sib[RIGHT] = [send(xall.at[RIGHT, 0, low], xall.at[RIGHT, 1, low], space=sibling)]

    ld_time.wait()
    time_t[...] = time_v[...].T.astype(BF16)
    for e in range(1, NTM):
        from_meta[e].wait_recv()

    @pl.loop(0, NTM // 2)
    def _(m):
        row = meta_in[2 * m, 0:1, :] + meta_in[2 * m + 1, 0:1, :]
        when = lax.shift_right_arithmetic(row, 3)
        which = jnp.bitwise_and(row, 7)
        hot = lax.broadcasted_iota(jnp.int32, (TIMES, 2 * SLOTS), 0) == when
        picked = nn_dot(time_t[...], jnp.where(hot, 1.0, 0.0).astype(BF16))
        slots = pl.ds(pl.multiple_of(m * 2 * SLOTS, 2 * SLOTS), 2 * SLOTS)
        picked_t = picked.T
        which_t = jnp.broadcast_to(which.astype(F32), (2 * SLOTS, 2 * SLOTS)).T
        for b in range(NBLK):
            gt4[b * ROWS : (b + 1) * ROWS, slots] = jnp.where(which == b, picked, 0.0).astype(BF16)
            g4[slots, b * ROWS : (b + 1) * ROWS] = jnp.where(
                which_t == float(b), picked_t, 0.0
            ).astype(BF16)

    from_sib[OWN][0].wait_recv()
    add_spread(OWN, 1)
    from_left1.wait_recv()
    from_sib[LEFT].append(send(xall.at[LEFT, 0, low], xall.at[LEFT, 1, low], space=sibling))
    from_right0.wait_recv()
    from_sib[RIGHT].append(send(xall.at[RIGHT, 0, top], xall.at[RIGHT, 1, top], space=sibling))
    add_spread(LEFT, 0)
    add_spread(RIGHT, 0)
    for rel in (LEFT, RIGHT):
        for copy in from_sib[rel]:
            copy.wait_recv()
        add_spread(rel, 1)
    from_opp0.wait_recv()
    from_sib[OPP] = [send(xall.at[OPP, 0, top], xall.at[OPP, 1, top], space=sibling)]
    from_opp1.wait_recv()
    from_sib[OPP].append(send(xall.at[OPP, 0, low], xall.at[OPP, 1, low], space=sibling))
    add_spread(OPP, 0)
    for copy in from_sib[OPP]:
        copy.wait_recv()
    add_spread(OPP, 1)

    spread4 = jnp.concatenate(
        [spread_v[:, b * BLK : (b + 1) * BLK].astype(BF16) for b in range(NBLK)], axis=0
    )
    from_part = [None] * NTM
    for m in range(NTM // 2):
        part = nn_dot(g4[m * 2 * SLOTS : (m + 1) * 2 * SLOTS, :], spread4)
        part_out[2 * m : 2 * m + 2] = part.astype(BF16).reshape(2, SLOTS, BLK)
        for e in (2 * m, 2 * m + 1):
            if e:
                from_part[e] = send(part_out.at[e], part_in.at[e], tm=minus(e))
    flux = part_out[0].astype(F32)
    for e in range(1, NTM):
        from_part[e].wait_recv()
        flux += part_in[e].astype(F32)
    flux = flux.astype(BF16)

    ld_foot.wait()
    ld_obs.wait()
    group = 16
    row16 = lax.broadcasted_iota(jnp.int32, (group, BLK), 0)
    for g in range(SLOTS // group):
        mine = flux[g * group : (g + 1) * group, :]
        acc = jnp.zeros((group, OBS), F32)
        for k in range(group):
            acc += nt_dot(jnp.where(row16 == k, mine, jnp.zeros_like(mine)), foot_v[g * group + k])
        sims_v[g * group : (g + 1) * group, :] = acc
    sims = sims_v[...]
    pick = jnp.where(
        lax.broadcasted_iota(jnp.int32, (SLOTS, SLOTS), 0) == obs_v[...] - tm * SLOTS, 1.0, 0.0
    )
    pick_low = pick.astype(BF16)
    sims_hi = sims.astype(BF16)
    sims_lo = (sims - sims_hi.astype(F32)).astype(BF16)
    evolved = nn_dot(pick_low, sims_hi) + nn_dot(pick_low, sims_lo)
    evo_out[...] = evolved.astype(BF16)
    from_evo = [None] + [
        send(evo_out, evo_in.at[d], space=lax.rem(sp + d, NSP)) for d in range(1, NSP)
    ]
    pick_t = pick.T.astype(BF16)
    ld_dep.wait()
    ld_weight.wait()
    for d in range(1, NSP):
        from_evo[d].wait_recv()
        evolved += evo_in[d].astype(F32)
    depart = (weight_v[...] * (evolved - dep_v[...])).astype(BF16)
    mine_dep = nn_dot(pick_t, depart).astype(BF16)

    row16 = lax.broadcasted_iota(jnp.int32, (group, OBS), 0)
    for g in range(SLOTS // group):
        mine = mine_dep[g * group : (g + 1) * group, :]
        acc = jnp.zeros((group, BLK), F32)
        for k in range(group):
            acc += nn_dot(jnp.where(row16 == k, mine, jnp.zeros_like(mine)), foot_v[g * group + k])
        back_out[g * group : (g + 1) * group, :] = acc.astype(BF16)
    from_back = [None] + [send(back_out, back_in.at[e], tm=plus(e)) for e in range(1, NTM)]
    back_in[0] = back_out[...]

    adj = jnp.zeros((NBLK * ROWS, BLK), F32)
    for q in range(4):
        for e in range(4 * q, 4 * q + 4):
            if e:
                from_back[e].wait_recv()
        adj += nn_dot(
            gt4[:, q * 4 * SLOTS : (q + 1) * 4 * SLOTS],
            back_in[4 * q : 4 * q + 4].reshape(4 * SLOTS, BLK),
        )
    for b in range(NBLK):
        adj_v[:, b * BLK : (b + 1) * BLK] = adj[b * ROWS : (b + 1) * ROWS, :].astype(BF16)

    def terms(rel, c, out):
        @pl.loop(0, COLS // BLK)
        def _(n):
            cols = pl.ds(pl.multiple_of(n * BLK, BLK), BLK)
            out[:, cols] = nn_dot(adj_v[...], space_v[rel, c, :, cols]).astype(out.dtype)

    from_pair = {}

    def to_sibling(rel):
        terms(rel, 1, sib_out.at[rel])
        from_pair[rel] = send(sib_out.at[rel], sib_in.at[rel], space=sibling)

    def pair(rel, rows):
        return term_v[rel, rows, :] + sib_in[rel, rows, :].astype(F32)

    to_sibling(OPP)
    terms(OPP, 0, term_v.at[OPP])
    to_sibling(LEFT)
    from_pair[OPP].wait_recv()
    hop_out[0] = pair(OPP, top).astype(BF16)
    far_left = send(hop_out.at[0], hop_in.at[0], space=right)
    hop_out[1] = pair(OPP, low).astype(BF16)
    far_right = send(hop_out.at[1], hop_in.at[1], space=left)
    to_sibling(RIGHT)
    terms(LEFT, 0, term_v.at[LEFT])
    from_pair[LEFT].wait_recv()
    hop_out[2] = pair(LEFT, top).astype(BF16)
    near_right = send(hop_out.at[2], hop_in.at[2], space=left)
    terms(RIGHT, 0, term_v.at[RIGHT])
    from_pair[RIGHT].wait_recv()
    hop_out[3] = pair(RIGHT, low).astype(BF16)
    near_left = send(hop_out.at[3], hop_in.at[3], space=right)
    to_sibling(OWN)
    far_left.wait_recv()
    hop_out[4] = (pair(RIGHT, top) + hop_in[0].astype(F32)).astype(BF16)
    last_left = send(hop_out.at[4], hop_in.at[4], space=right)
    far_right.wait_recv()
    hop_out[5] = (pair(LEFT, low) + hop_in[1].astype(F32)).astype(BF16)
    last_right = send(hop_out.at[5], hop_in.at[5], space=left)
    terms(OWN, 0, term_v.at[OWN])
    from_pair[OWN].wait_recv()
    out_v[...] = state_v[...] + term_v[OWN] + sib_in[OWN].astype(F32)
    near_right.wait_recv()
    out_v[top, :] += hop_in[2].astype(F32)
    near_left.wait_recv()
    out_v[low, :] += hop_in[3].astype(F32)
    last_left.wait_recv()
    out_v[top, :] += hop_in[4].astype(F32)
    out0 = pltpu.make_async_copy(out_v.at[top], out_hbm.at[top], lsem.at[len(loads)])
    out0.start()
    last_right.wait_recv()
    out_v[low, :] += hop_in[5].astype(F32)
    out1 = pltpu.make_async_copy(out_v.at[low], out_hbm.at[low], lsem.at[len(loads) + 1])
    out1.start()
    for copy in sends:
        copy.wait_send()
    out0.wait()
    out1.wait()


N_LOADS = 18
N_SENDS = 15 + 6 + 7 + 15 + 7 + 15 + 4 + 6


def local(
    state,
    space_factor,
    time_factor,
    footprints,
    tile_obs,
    tile_block,
    tile_time,
    tile_count,
    obs_dep,
    obs_weight,
):
    any_spec = pl.BlockSpec(memory_space=pl.ANY)
    vm = pltpu.VMEM
    return pl.pallas_call(
        kernel,
        out_shape=jax.ShapeDtypeStruct((ROWS, COLS), F32),
        in_specs=[any_spec] * 10,
        out_specs=any_spec,
        scratch_shapes=[
            vm((ROWS, COLS), F32),
            vm((NX, 2, COLS, COLS), BF16),
            vm((TIMES, ROWS), F32),
            vm((SLOTS, OBS, BLK), BF16),
            vm((1, SLOTS), jnp.int32),
            vm((1, SLOTS), jnp.int32),
            vm((1, SLOTS), jnp.int32),
            vm((1, 1), jnp.int32),
            vm((SLOTS, OBS), F32),
            vm((SLOTS, OBS), F32),
            vm((ROWS, COLS), F32),
            vm((NX, 2, ROWS, COLS), BF16),
            vm((ROWS, COLS), F32),
            vm((ROWS, TIMES), BF16),
            vm((2, 8, 2 * SLOTS), jnp.int32),
            vm((NTM, 8, 2 * SLOTS), jnp.int32),
            vm((NBLK * ROWS, NTM * SLOTS), BF16),
            vm((NTM * SLOTS, NBLK * ROWS), BF16),
            vm((NTM, SLOTS, BLK), BF16),
            vm((NTM, SLOTS, BLK), BF16),
            vm((SLOTS, OBS), F32),
            vm((SLOTS, OBS), BF16),
            vm((NSP, SLOTS, OBS), BF16),
            vm((SLOTS, BLK), BF16),
            vm((NTM, SLOTS, BLK), BF16),
            vm((ROWS, COLS), BF16),
            vm((NX, ROWS, COLS), BF16),
            vm((NX, ROWS, COLS), BF16),
            vm((NX, ROWS, COLS), F32),
            vm((6, HALF, COLS), BF16),
            vm((6, HALF, COLS), BF16),
            pltpu.SemaphoreType.DMA((N_LOADS + 2,)),
            pltpu.SemaphoreType.DMA((N_SENDS,)),
            pltpu.SemaphoreType.DMA((N_SENDS,)),
        ],
        compiler_params=pltpu.CompilerParams(
            collective_id=0, has_side_effects=True, vmem_limit_bytes=56 * 1024 * 1024
        ),
    )(
        state,
        space_factor,
        time_factor,
        footprints.reshape(SLOTS, OBS, BLK),
        tile_obs.reshape(1, SLOTS),
        tile_block.reshape(1, SLOTS),
        tile_time.reshape(1, SLOTS),
        tile_count,
        obs_dep,
        obs_weight,
    )


def solution(mesh):
    return jax.shard_map(
        local,
        mesh=mesh,
        in_specs=(
            P("tm", "space"),
            P("space", None),
            P(),
            P("tm", "space", None, None),
            P("tm", "space"),
            P("tm", "space"),
            P("tm", "space"),
            P("tm", "space"),
            P("tm", None),
            P("tm", None),
        ),
        out_specs=P("tm", "space"),
        check_vma=False,
    )
```

time: 388 us -> 70 us (0.18)
  waiting for transfers between devices: 195 us -> 0 us
  matrix products: 122 us -> 0 us
  Pallas kernels: 0 us -> 67.3 us
  blocking collectives: 25.6 us -> 0 us
  local copies, waits for them, and re-layouts: 19 us -> 1.89 us
  between operations: 13.9 us -> 0.66 us
  other arithmetic: 11.1 us -> 0 us
    dot_general x7 -> x0, matrix products: 122 us -> none  [the longest x1 57.1 us: local(): lax.dot_general(factor_cols, q_part, (((0,), (0,)), ((), ())), precision=...]
    reduce_scatter x2 -> x0, waiting for transfers between devices: 115 us -> none  [the longest x1 82.6 us: local(): lax.psum_scatter(lax.dot_general(factor_cols, q_part, (((0,), (0,)), ((),...]
    all_gather x2 -> x0, waiting for transfers between devices: 79.4 us -> none  [the longest x1 51.2 us: local(): lax.all_gather(spread.astype(jnp.bfloat16), 'tm', axis=0, tiled=True)]
    pallas_call x0 -> x1, Pallas kernels: none -> 67.3 us  [local(): pl.pallas_call(kernel, out_shape=jax.ShapeDtypeStruct((ROWS, COLS), F32),...]
    psum x1 -> x0, blocking collectives: 25.6 us -> none  [local(): lax.psum(sim_part.astype(jnp.bfloat16), 'space').astype(jnp.float32)]
    reshape x1 -> x0, local copies, waits for them, and re-layouts: 7.46 us -> none  [local(): flux.astype(jnp.bfloat16).reshape(all_times, local_blocks, block_cells)]
    scatter-add x1 -> x0, other arithmetic: 7.38 us -> none  [local(): q_part = jnp.zeros((all_times, local_blocks, block_cells), jnp.float32).a...]
  transfers between devices with their start and end apart: 4 -> 0, of which waited for: 4 -> 0; matrix products, arithmetic and copies ran while one was open for 0% -> 0% of each run, Pallas kernels for 0% -> 0%
where the time goes in v1:
time: 70 us; the launch traced here: 69.9 us
  Pallas kernels  67.3 us (96%)
  local copies, waits for them, and re-layouts  1.89 us (3%)
    pallas_call x1, Pallas kernels, local(): pl.pallas_call(kernel, out_shape=jax.ShapeDtypeStruct((ROWS, COLS), F32),...  67.3 us
    unnamed x1, local copies, waits for them, and re-layouts  1.89 us

profile of v1, /device:TPU:0, one launch (start us, length us, event | category | flops | bytes accessed | tf_op | source)
XLA Modules:
  0.0 69.9 jit_solution(17797770324858330465)
XLA Ops:
  0.7 67.3 %shard_map.100 = f32[128,1024]{1,0:T(8,128)} custom-call(f32[128,1024]{1,0:T(8,128)} %state_hbm.1, bf16[1024,8192]{1,0:T(8,128)(2,1)} %space_hbm.1, f32[2048,2048]{1,0:T(8,128)} %time_hbm.1, bf16[64,128,256]{2,1,0:T(8,128)(2,1)} %bitcast.4, s32[1,64]{1,0:T(1,128)} %bitcast.5, s32[1,64]{1,0:T(1,128)} %bitcast.6, s32[1,64]{1,0:T(1,128)} %bitcast.7, ...), custom_call_target="tpu_custom_call" | custom-call | tf_op jit(solution)/shard_map/pallas_call | solution.py:387
  68.0 1.9 %copy.13 = f32[128,1024]{1,0:T(8,128)} copy(f32[128,1024]{1,0:T(8,128)} %shard_map.100) | data formatting | bytes 1048576

commit v2 on v1

v2 whole, which is shorter than its diff:
```python
import functools

import jax
import jax.numpy as jnp
from jax import lax
from jax.experimental import pallas as pl
from jax.experimental.pallas import tpu as pltpu
from jax.sharding import PartitionSpec as P

MESH = pl.DeviceIdType.MESH
F32 = jnp.float32
BF16 = jnp.bfloat16
NX = 4
NTM = 16
NSP = 8
SLOTS = 64
ROWS = 128
COLS = 1024
HALF = COLS // 2
BLK = 256
NBLK = COLS // BLK
OBS = 128
TIMES = 2048
OWN, RIGHT, OPP, LEFT = 0, 1, 2, 3


FAR_FIRST = (10, 11, 6, 9, 14, 2, 8, 7, 5, 13, 15, 3, 1, 12, 4)


def nt_dot(a, b):
    return lax.dot_general(a, b, (((1,), (1,)), ((), ())), preferred_element_type=F32)


def nn_dot(a, b):
    return jnp.dot(a, b, preferred_element_type=F32)


def kernel(
    state_hbm,
    space_hbm,
    time_hbm,
    foot_hbm,
    obs_hbm,
    block_hbm,
    when_hbm,
    count_hbm,
    dep_hbm,
    weight_hbm,
    out_hbm,
    state_v,
    space_v,
    time_v,
    foot_v,
    foot_t,
    obs_v,
    block_v,
    when_v,
    count_v,
    dep_v,
    weight_v,
    out_v,
    xall,
    spread_v,
    time_t,
    meta_out,
    meta_y,
    line_out,
    meta_z,
    gt,
    gt4,
    g4,
    part_out,
    part_in,
    sims_v,
    evo_out,
    evo_in,
    back_out,
    back_in,
    adj_v,
    sib_out,
    sib_in,
    term_v,
    hop_out,
    hop_in,
    lsem,
    ssem,
    rsem,
):
    tm = lax.axis_index("tm")
    sp = lax.axis_index("space")
    z, y = lax.div(tm, NX), lax.rem(tm, NX)
    x, core = lax.div(sp, 2), lax.rem(sp, 2)
    other = 1 - core

    def at_x(rel, c):
        return lax.rem(x + rel, NX) * 2 + (other if c else core)

    def plus(e):
        dz, dy = divmod(e, NX)
        return lax.rem(z + dz, NX) * NX + lax.rem(y + dy, NX)

    def minus(e):
        dz, dy = divmod(e, NX)
        return lax.rem(z + NX - dz, NX) * NX + lax.rem(y + NX - dy, NX)

    loads = []

    def load(src, dst):
        copy = pltpu.make_async_copy(src, dst, lsem.at[len(loads)])
        copy.start()
        loads.append(copy)
        return copy

    sends = []

    def send(src, dst, **where):
        n = len(sends)
        copy = pltpu.make_async_remote_copy(
            src_ref=src,
            dst_ref=dst,
            send_sem=ssem.at[n],
            recv_sem=rsem.at[n],
            device_id=where,
            device_id_type=MESH,
        )
        copy.start()
        sends.append(copy)
        return copy

    right, left = at_x(RIGHT, 0), at_x(LEFT, 0)
    sibling = at_x(OWN, 1)

    ld_state = load(state_hbm, state_v)
    ld_when = load(when_hbm, when_v)
    ld_block = load(block_hbm, block_v)
    ld_count = load(count_hbm, count_v)
    barrier = pltpu.get_barrier_semaphore()
    for d in (sibling, right, left):
        pl.semaphore_signal(barrier, inc=1, device_id={"space": d}, device_id_type=MESH)
    for e in (2, 1, 3, 2 * NX, NX, 3 * NX):
        pl.semaphore_signal(barrier, inc=1, device_id={"tm": plus(e)}, device_id_type=MESH)

    ld_state.wait()
    ld_space = {}

    def load_space(rel, c):
        cols = pl.ds(pl.multiple_of(at_x(rel, c) * COLS, COLS), COLS)
        ld_space[rel, c] = load(space_hbm.at[:, cols], space_v.at[rel, c])

    load_space(OWN, 0)
    load_space(OWN, 1)
    ld_time = load(time_hbm.at[:, pl.ds(pl.multiple_of(tm * ROWS, ROWS), ROWS)], time_v)
    for rel in (LEFT, RIGHT, OPP):
        load_space(rel, 0)
        load_space(rel, 1)
    ld_foot = load(foot_hbm, foot_v)
    ld_obs = load(obs_hbm, obs_v)
    ld_dep = load(dep_hbm, dep_v)
    ld_weight = load(weight_hbm, weight_v)

    for h in range(2):
        xall[OWN, 0, h] = state_v[:, h * HALF : (h + 1) * HALF].astype(BF16)
    ld_when.wait()
    ld_block.wait()
    ld_count.wait()
    lane = lax.broadcasted_iota(jnp.int32, (1, SLOTS), 1)
    code = when_v[...] * 8 + (block_v[...] - sp * NBLK)
    code = jnp.where(lane < count_v[...], code, -8)
    zero = jnp.zeros((1, SLOTS), jnp.int32)
    meta_out[0] = jnp.broadcast_to(jnp.concatenate([code, zero], axis=1), (8, 2 * SLOTS))
    meta_out[1] = jnp.broadcast_to(jnp.concatenate([zero, code], axis=1), (8, 2 * SLOTS))
    pl.semaphore_wait(barrier, 9)

    def block_to(rel, at, h, where):
        return send(xall.at[rel, 0, h], xall.at[at, 0, h], space=where)

    def block_over(rel, h):
        return send(xall.at[rel, 0, h], xall.at[rel, 1, h], space=sibling)

    got = {}
    got[LEFT, 0, 0] = block_to(OWN, LEFT, 0, right)
    got[RIGHT, 0, 1] = block_to(OWN, RIGHT, 1, left)
    from_y = [None] + [send(meta_out.at[d % 2], meta_y.at[d], tm=plus(d)) for d in range(1, NX)]
    got[LEFT, 0, 1] = block_to(OWN, LEFT, 1, right)
    got[RIGHT, 0, 0] = block_to(OWN, RIGHT, 0, left)
    for h in range(2):
        got[OWN, 1, h] = block_over(OWN, h)

    def add_spread(rel, c, h, first=False):
        term = nt_dot(xall[rel, c, h], space_v[rel, c, :, h * HALF : (h + 1) * HALF])
        if first:
            spread_v[...] = term
        else:
            spread_v[...] += term

    ld_space[OWN, 0].wait()
    add_spread(OWN, 0, 0, first=True)
    add_spread(OWN, 0, 1)
    for d in range(1, NX):
        from_y[d].wait_recv()
    line_out[0] = meta_out[0] + meta_y[1]
    line_out[1] = meta_y[2] + meta_y[3]
    from_z = [None] + [send(line_out, meta_z.at[d], tm=plus(d * NX)) for d in range(1, NX)]
    meta_z[0] = line_out[...]
    ld_space[OWN, 1].wait()
    for h in range(2):
        got[OWN, 1, h].wait_recv()
        add_spread(OWN, 1, h)
    ld_time.wait()
    time_t[...] = time_v[...].T.astype(BF16)
    got[LEFT, 0, 0].wait_recv()
    got[OPP, 0, 0] = block_to(LEFT, OPP, 0, right)
    got[RIGHT, 0, 1].wait_recv()
    got[OPP, 0, 1] = block_to(RIGHT, OPP, 1, left)
    got[LEFT, 1, 0] = block_over(LEFT, 0)
    got[RIGHT, 1, 1] = block_over(RIGHT, 1)

    for d in range(1, NX):
        from_z[d].wait_recv()

    @pl.loop(0, NX)
    def _(d):
        row = jnp.concatenate([meta_z[d, 0, 0:1, :], meta_z[d, 1, 0:1, :]], axis=1)
        when = lax.shift_right_arithmetic(row, 3)
        which = jnp.bitwise_and(row, 7)
        hot = lax.broadcasted_iota(jnp.int32, (TIMES, NX * SLOTS), 0) == when
        picked = nn_dot(time_t[...], jnp.where(hot, 1.0, 0.0).astype(BF16))
        slots = pl.ds(pl.multiple_of(d * NX * SLOTS, NX * SLOTS), NX * SLOTS)
        gt[:, slots] = picked.astype(BF16)
        picked_t = picked.T
        which_t = jnp.broadcast_to(which.astype(F32), (ROWS, NX * SLOTS)).T
        for b in range(NBLK):
            g4[slots, b * ROWS : (b + 1) * ROWS] = jnp.where(
                which_t == float(b), picked_t, 0.0
            ).astype(BF16)

    for rel, c, h in ((LEFT, 0, 0), (RIGHT, 0, 1), (LEFT, 1, 0), (RIGHT, 1, 1)):
        if h == (rel == RIGHT) and c == 0:
            ld_space[rel, 0].wait()
            ld_space[rel, 1].wait()
        if c:
            got[rel, c, h].wait_recv()
        add_spread(rel, c, h)
    for rel, h in ((LEFT, 1), (RIGHT, 0)):
        got[rel, 0, h].wait_recv()
        got[rel, 1, h] = block_over(rel, h)
    for rel, h in ((LEFT, 1), (RIGHT, 0)):
        add_spread(rel, 0, h)
    for rel, h in ((LEFT, 1), (RIGHT, 0)):
        got[rel, 1, h].wait_recv()
        add_spread(rel, 1, h)
    ld_space[OPP, 0].wait()
    ld_space[OPP, 1].wait()
    for h in range(2):
        got[OPP, 0, h].wait_recv()
        got[OPP, 1, h] = block_over(OPP, h)
    for c in range(2):
        for h in range(2):
            if c:
                got[OPP, 1, h].wait_recv()
            add_spread(OPP, c, h)

    spread4 = jnp.concatenate(
        [spread_v[:, b * BLK : (b + 1) * BLK].astype(BF16) for b in range(NBLK)], axis=0
    )
    from_part = [None] * NTM
    done = set()
    for e in FAR_FIRST + (0,):
        m = e // 2
        if m not in done:
            done.add(m)
            part = nn_dot(g4[m * 2 * SLOTS : (m + 1) * 2 * SLOTS, :], spread4)
            part_out[2 * m : 2 * m + 2] = part.astype(BF16).reshape(2, SLOTS, BLK)
        if e:
            from_part[e] = send(part_out.at[e], part_in.at[e], tm=minus(e))

    for b in range(NBLK):
        for d in range(NX):
            which = jnp.bitwise_and(
                jnp.concatenate([meta_z[d, 0, 0:1, :], meta_z[d, 1, 0:1, :]], axis=1), 7
            )
            slots = slice(d * NX * SLOTS, (d + 1) * NX * SLOTS)
            gt4[b * ROWS : (b + 1) * ROWS, slots] = jnp.where(
                which == b, gt[:, slots].astype(F32), 0.0
            ).astype(BF16)
    ld_foot.wait()

    @pl.loop(0, SLOTS // 4)
    def _(k):
        for i in range(4):
            foot_t[4 * k + i] = foot_v[4 * k + i].T

    ld_obs.wait()
    pick = jnp.where(
        lax.broadcasted_iota(jnp.int32, (SLOTS, SLOTS), 0) == obs_v[...] - tm * SLOTS, 1.0, 0.0
    )
    pick_low = pick.astype(BF16)
    pick_t = pick.T.astype(BF16)
    ld_dep.wait()
    ld_weight.wait()

    flux = part_out[0].astype(F32)
    for e in FAR_FIRST[::-1]:
        from_part[e].wait_recv()
        flux += part_in[e].astype(F32)
    flux = flux.astype(BF16)

    group = 16
    row16 = lax.broadcasted_iota(jnp.int32, (group, BLK), 0)
    for g in range(SLOTS // group):
        mine = flux[g * group : (g + 1) * group, :]
        acc = jnp.zeros((group, OBS), F32)
        for k in range(group):
            acc += nn_dot(jnp.where(row16 == k, mine, jnp.zeros_like(mine)), foot_t[g * group + k])
        sims_v[g * group : (g + 1) * group, :] = acc
    sims = sims_v[...]
    sims_hi = sims.astype(BF16)
    sims_lo = (sims - sims_hi.astype(F32)).astype(BF16)
    evolved = nn_dot(pick_low, sims_hi) + nn_dot(pick_low, sims_lo)
    evo_out[...] = evolved.astype(BF16)
    from_evo = []
    for rel, c in ((OPP, 1), (OPP, 0), (RIGHT, 1), (LEFT, 1), (RIGHT, 0), (LEFT, 0), (OWN, 1)):
        from_evo.append(send(evo_out, evo_in.at[len(from_evo)], space=at_x(rel, c)))
    for n in range(NSP - 1)[::-1]:
        from_evo[n].wait_recv()
        evolved += evo_in[n].astype(F32)
    depart = (weight_v[...] * (evolved - dep_v[...])).astype(BF16)
    mine_dep = nn_dot(pick_t, depart).astype(BF16)

    row16 = lax.broadcasted_iota(jnp.int32, (group, OBS), 0)
    for g in range(SLOTS // group):
        mine = mine_dep[g * group : (g + 1) * group, :]
        acc = jnp.zeros((group, BLK), F32)
        for k in range(group):
            acc += nn_dot(jnp.where(row16 == k, mine, jnp.zeros_like(mine)), foot_v[g * group + k])
        back_out[g * group : (g + 1) * group, :] = acc.astype(BF16)
    from_back = [None] * NTM
    for e in FAR_FIRST:
        from_back[e] = send(back_out, back_in.at[e], tm=plus(e))
    back_in[0] = back_out[...]

    adj = jnp.zeros((NBLK * ROWS, BLK), F32)
    for q in (0, 1, 3, 2):
        for e in range(4 * q, 4 * q + 4):
            if e:
                from_back[e].wait_recv()
        adj += nn_dot(
            gt4[:, q * 4 * SLOTS : (q + 1) * 4 * SLOTS],
            back_in[4 * q : 4 * q + 4].reshape(4 * SLOTS, BLK),
        )
    for b in range(NBLK):
        adj_v[:, b * BLK : (b + 1) * BLK] = adj[b * ROWS : (b + 1) * ROWS, :].astype(BF16)

    def terms(rel, c, h):
        return nn_dot(adj_v[...], space_v[rel, c, :, h * HALF : (h + 1) * HALF])

    from_pair = {}

    def to_sibling(rel, h):
        sib_out[rel, h] = terms(rel, 1, h).astype(BF16)
        from_pair[rel, h] = send(sib_out.at[rel, h], sib_in.at[rel, h], space=sibling)

    def own_terms(rel, h):
        term_v[rel, h] = terms(rel, 0, h)

    def pair(rel, h):
        from_pair[rel, h].wait_recv()
        return term_v[rel, h] + sib_in[rel, h].astype(F32)

    def hop(n, value, where):
        hop_out[n] = value.astype(BF16)
        return send(hop_out.at[n], hop_in.at[n], space=where)

    to_sibling(OPP, 0)
    to_sibling(OPP, 1)
    own_terms(OPP, 0)
    own_terms(OPP, 1)
    to_sibling(LEFT, 0)
    to_sibling(RIGHT, 1)
    far_left = hop(0, pair(OPP, 0), right)
    far_right = hop(1, pair(OPP, 1), left)
    own_terms(LEFT, 0)
    own_terms(RIGHT, 1)
    near_right = hop(2, pair(LEFT, 0), left)
    near_left = hop(3, pair(RIGHT, 1), right)
    to_sibling(RIGHT, 0)
    to_sibling(LEFT, 1)
    own_terms(RIGHT, 0)
    own_terms(LEFT, 1)
    term_v[RIGHT, 0] = pair(RIGHT, 0)
    term_v[LEFT, 1] = pair(LEFT, 1)
    far_left.wait_recv()
    last_left = hop(4, term_v[RIGHT, 0] + hop_in[0].astype(F32), right)
    far_right.wait_recv()
    last_right = hop(5, term_v[LEFT, 1] + hop_in[1].astype(F32), left)
    to_sibling(OWN, 0)
    to_sibling(OWN, 1)
    own_terms(OWN, 0)
    own_terms(OWN, 1)
    for h in range(2):
        cols = slice(h * HALF, (h + 1) * HALF)
        out_v[:, cols] = state_v[:, cols] + pair(OWN, h)
    near_right.wait_recv()
    out_v[:, :HALF] += hop_in[2].astype(F32)
    near_left.wait_recv()
    out_v[:, HALF:] += hop_in[3].astype(F32)
    outs = []
    for h, copy in enumerate((last_left, last_right)):
        cols = slice(h * HALF, (h + 1) * HALF)
        copy.wait_recv()
        out_v[:, cols] += hop_in[4 + h].astype(F32)
        outs.append(load(out_v.at[:, cols], out_hbm.at[:, cols]))
    for copy in sends:
        copy.wait_send()
    for copy in outs:
        copy.wait()


N_LOADS = 20
N_SENDS = 3 + 3 + 6 + 8 + 15 + 7 + 15 + 8 + 6


def local(
    state,
    space_factor,
    time_factor,
    footprints,
    tile_obs,
    tile_block,
    tile_time,
    tile_count,
    obs_dep,
    obs_weight,
):
    any_spec = pl.BlockSpec(memory_space=pl.ANY)
    vm = pltpu.VMEM
    i32 = jnp.int32
    return pl.pallas_call(
        kernel,
        out_shape=jax.ShapeDtypeStruct((ROWS, COLS), F32),
        in_specs=[any_spec] * 10,
        out_specs=any_spec,
        scratch_shapes=[
            vm((ROWS, COLS), F32),
            vm((NX, 2, COLS, COLS), BF16),
            vm((TIMES, ROWS), F32),
            vm((SLOTS, OBS, BLK), BF16),
            vm((SLOTS, BLK, OBS), BF16),
            vm((1, SLOTS), i32),
            vm((1, SLOTS), i32),
            vm((1, SLOTS), i32),
            vm((1, 1), i32),
            vm((SLOTS, OBS), F32),
            vm((SLOTS, OBS), F32),
            vm((ROWS, COLS), F32),
            vm((NX, 2, 2, ROWS, HALF), BF16),
            vm((ROWS, COLS), F32),
            vm((ROWS, TIMES), BF16),
            vm((2, 8, 2 * SLOTS), i32),
            vm((NX, 8, 2 * SLOTS), i32),
            vm((2, 8, 2 * SLOTS), i32),
            vm((NX, 2, 8, 2 * SLOTS), i32),
            vm((ROWS, NTM * SLOTS), BF16),
            vm((NBLK * ROWS, NTM * SLOTS), BF16),
            vm((NTM * SLOTS, NBLK * ROWS), BF16),
            vm((NTM, SLOTS, BLK), BF16),
            vm((NTM, SLOTS, BLK), BF16),
            vm((SLOTS, OBS), F32),
            vm((SLOTS, OBS), BF16),
            vm((NSP - 1, SLOTS, OBS), BF16),
            vm((SLOTS, BLK), BF16),
            vm((NTM, SLOTS, BLK), BF16),
            vm((ROWS, COLS), BF16),
            vm((NX, 2, ROWS, HALF), BF16),
            vm((NX, 2, ROWS, HALF), BF16),
            vm((NX, 2, ROWS, HALF), F32),
            vm((6, ROWS, HALF), BF16),
            vm((6, ROWS, HALF), BF16),
            pltpu.SemaphoreType.DMA((N_LOADS,)),
            pltpu.SemaphoreType.DMA((N_SENDS,)),
            pltpu.SemaphoreType.DMA((N_SENDS,)),
        ],
        compiler_params=pltpu.CompilerParams(
            collective_id=0, has_side_effects=True, vmem_limit_bytes=56 * 1024 * 1024
        ),
    )(
        state,
        space_factor,
        time_factor,
        footprints.reshape(SLOTS, OBS, BLK),
        tile_obs.reshape(1, SLOTS),
        tile_block.reshape(1, SLOTS),
        tile_time.reshape(1, SLOTS),
        tile_count,
        obs_dep,
        obs_weight,
    )


def solution(mesh):
    return jax.shard_map(
        local,
        mesh=mesh,
        in_specs=(
            P("tm", "space"),
            P("space", None),
            P(),
            P("tm", "space", None, None),
            P("tm", "space"),
            P("tm", "space"),
            P("tm", "space"),
            P("tm", "space"),
            P("tm", None),
            P("tm", None),
        ),
        out_specs=P("tm", "space"),
        check_vma=False,
    )
```

time: 70 us -> 61.1 us (0.87)
  Pallas kernels: 67.3 us -> 58 us
    pallas_call x1, Pallas kernels: 67.3 us -> 58 us  [local(): pl.pallas_call(kernel, out_shape=jax.ShapeDtypeStruct((ROWS, COLS), F32),...]
where the time goes in v2:
time: 61.1 us; the launch traced here: 60.6 us
  Pallas kernels  58 us (95%)
  local copies, waits for them, and re-layouts  1.89 us (3%)
  between operations  0.66 us (1%)
    pallas_call x1, Pallas kernels, local(): pl.pallas_call(kernel, out_shape=jax.ShapeDtypeStruct((ROWS, COLS), F32),...  58 us
    unnamed x1, local copies, waits for them, and re-layouts  1.89 us

profile of v2, /device:TPU:0, one launch (start us, length us, event | category | flops | bytes accessed | tf_op | source)
XLA Modules:
  0.0 60.6 jit_solution(4605740790142277890)
XLA Ops:
  0.7 58.0 %shard_map.100 = f32[128,1024]{1,0:T(8,128)} custom-call(f32[128,1024]{1,0:T(8,128)} %state_hbm.1, bf16[1024,8192]{1,0:T(8,128)(2,1)} %space_hbm.1, f32[2048,2048]{1,0:T(8,128)} %time_hbm.1, bf16[64,128,256]{2,1,0:T(8,128)(2,1)} %bitcast.4, s32[1,64]{1,0:T(1,128)} %bitcast.5, s32[1,64]{1,0:T(1,128)} %bitcast.6, s32[1,64]{1,0:T(1,128)} %bitcast.7, ...), custom_call_target="tpu_custom_call" | custom-call | tf_op jit(solution)/shard_map/pallas_call | solution.py:438
  58.7 1.9 %copy.13 = f32[128,1024]{1,0:T(8,128)} copy(f32[128,1024]{1,0:T(8,128)} %shard_map.100) | data formatting | bytes 1048576

commit v3 on v2

--- a/solution.py
+++ b/solution.py
@@ -46,7 +46,7 @@
     count_hbm,
     dep_hbm,
     weight_hbm,
-    out_hbm,
+    out_v,
     state_v,
     space_v,
     time_v,
@@ -58,7 +58,6 @@
     count_v,
     dep_v,
     weight_v,
-    out_v,
     xall,
     spread_v,
     time_t,
@@ -85,6 +84,8 @@
     lsem,
     ssem,
     rsem,
+    bssem,
+    brsem,
 ):
     tm = lax.axis_index("tm")
     sp = lax.axis_index("space")
@@ -180,7 +181,9 @@
     got = {}
     got[LEFT, 0, 0] = block_to(OWN, LEFT, 0, right)
     got[RIGHT, 0, 1] = block_to(OWN, RIGHT, 1, left)
-    from_y = [None] + [send(meta_out.at[d % 2], meta_y.at[d], tm=plus(d)) for d in range(1, NX)]
+    odd = lax.rem(y, 2)
+    from_y = [None] + [send(meta_out.at[odd], meta_y.at[y], tm=plus(d)) for d in range(1, NX)]
+    meta_y[y] = meta_out[odd]
     got[LEFT, 0, 1] = block_to(OWN, LEFT, 1, right)
     got[RIGHT, 0, 0] = block_to(OWN, RIGHT, 0, left)
     for h in range(2):
@@ -198,10 +201,10 @@
     add_spread(OWN, 0, 1)
     for d in range(1, NX):
         from_y[d].wait_recv()
-    line_out[0] = meta_out[0] + meta_y[1]
+    line_out[0] = meta_y[0] + meta_y[1]
     line_out[1] = meta_y[2] + meta_y[3]
-    from_z = [None] + [send(line_out, meta_z.at[d], tm=plus(d * NX)) for d in range(1, NX)]
-    meta_z[0] = line_out[...]
+    from_z = [None] + [send(line_out, meta_z.at[z], tm=plus(d * NX)) for d in range(1, NX)]
+    meta_z[z] = line_out[...]
     ld_space[OWN, 1].wait()
     for h in range(2):
         got[OWN, 1, h].wait_recv()
@@ -215,17 +218,29 @@
     got[LEFT, 1, 0] = block_over(LEFT, 0)
     got[RIGHT, 1, 1] = block_over(RIGHT, 1)
 
+    for rel, h in ((LEFT, 0), (RIGHT, 1)):
+        ld_space[rel, 0].wait()
+        add_spread(rel, 0, h)
+    for rel, h in ((LEFT, 1), (RIGHT, 0)):
+        got[rel, 0, h].wait_recv()
+        got[rel, 1, h] = block_over(rel, h)
+    for rel, h in ((LEFT, 0), (RIGHT, 1)):
+        ld_space[rel, 1].wait()
+        got[rel, 1, h].wait_recv()
+        add_spread(rel, 1, h)
+    for rel, h in ((LEFT, 1), (RIGHT, 0)):
+        add_spread(rel, 0, h)
+
     for d in range(1, NX):
         from_z[d].wait_recv()
 
-    @pl.loop(0, NX)
-    def _(d):
+    for d in range(NX):
         row = jnp.concatenate([meta_z[d, 0, 0:1, :], meta_z[d, 1, 0:1, :]], axis=1)
         when = lax.shift_right_arithmetic(row, 3)
         which = jnp.bitwise_and(row, 7)
         hot = lax.broadcasted_iota(jnp.int32, (TIMES, NX * SLOTS), 0) == when
         picked = nn_dot(time_t[...], jnp.where(hot, 1.0, 0.0).astype(BF16))
-        slots = pl.ds(pl.multiple_of(d * NX * SLOTS, NX * SLOTS), NX * SLOTS)
+        slots = slice(d * NX * SLOTS, (d + 1) * NX * SLOTS)
         gt[:, slots] = picked.astype(BF16)
         picked_t = picked.T
         which_t = jnp.broadcast_to(which.astype(F32), (ROWS, NX * SLOTS)).T
@@ -234,27 +249,14 @@
                 which_t == float(b), picked_t, 0.0
             ).astype(BF16)
 
-    for rel, c, h in ((LEFT, 0, 0), (RIGHT, 0, 1), (LEFT, 1, 0), (RIGHT, 1, 1)):
-        if h == (rel == RIGHT) and c == 0:
-            ld_space[rel, 0].wait()
-            ld_space[rel, 1].wait()
-        if c:
-            got[rel, c, h].wait_recv()
-        add_spread(rel, c, h)
-    for rel, h in ((LEFT, 1), (RIGHT, 0)):
-        got[rel, 0, h].wait_recv()
-        got[rel, 1, h] = block_over(rel, h)
-    for rel, h in ((LEFT, 1), (RIGHT, 0)):
-        add_spread(rel, 0, h)
+    for h in range(2):
+        got[OPP, 0, h].wait_recv()
+        got[OPP, 1, h] = block_over(OPP, h)
     for rel, h in ((LEFT, 1), (RIGHT, 0)):
         got[rel, 1, h].wait_recv()
         add_spread(rel, 1, h)
-    ld_space[OPP, 0].wait()
-    ld_space[OPP, 1].wait()
-    for h in range(2):
-        got[OPP, 0, h].wait_recv()
-        got[OPP, 1, h] = block_over(OPP, h)
     for c in range(2):
+        ld_space[OPP, c].wait()
         for h in range(2):
             if c:
                 got[OPP, 1, h].wait_recv()
@@ -263,16 +265,12 @@
     spread4 = jnp.concatenate(
         [spread_v[:, b * BLK : (b + 1) * BLK].astype(BF16) for b in range(NBLK)], axis=0
     )
+    for m in range(NTM // 2):
+        part = nn_dot(g4[m * 2 * SLOTS : (m + 1) * 2 * SLOTS, :], spread4)
+        part_out[2 * m : 2 * m + 2] = part.astype(BF16).reshape(2, SLOTS, BLK)
     from_part = [None] * NTM
-    done = set()
-    for e in FAR_FIRST + (0,):
-        m = e // 2
-        if m not in done:
-            done.add(m)
-            part = nn_dot(g4[m * 2 * SLOTS : (m + 1) * 2 * SLOTS, :], spread4)
-            part_out[2 * m : 2 * m + 2] = part.astype(BF16).reshape(2, SLOTS, BLK)
-        if e:
-            from_part[e] = send(part_out.at[e], part_in.at[e], tm=minus(e))
+    for e in FAR_FIRST:
+        from_part[e] = send(part_out.at[minus(e)], part_in.at[e], tm=minus(e))
 
     for b in range(NBLK):
         for d in range(NX):
@@ -299,7 +297,7 @@
     ld_dep.wait()
     ld_weight.wait()
 
-    flux = part_out[0].astype(F32)
+    flux = part_out[tm].astype(F32)
     for e in FAR_FIRST[::-1]:
         from_part[e].wait_recv()
         flux += part_in[e].astype(F32)
@@ -334,16 +332,32 @@
         for k in range(group):
             acc += nn_dot(jnp.where(row16 == k, mine, jnp.zeros_like(mine)), foot_v[g * group + k])
         back_out[g * group : (g + 1) * group, :] = acc.astype(BF16)
-    from_back = [None] * NTM
-    for e in FAR_FIRST:
-        from_back[e] = send(back_out, back_in.at[e], tm=plus(e))
-    back_in[0] = back_out[...]
+    def back_copy(dest, source):
+        return pltpu.make_async_remote_copy(
+            src_ref=back_out,
+            dst_ref=back_in.at[source],
+            send_sem=bssem.at[dest],
+            recv_sem=brsem.at[source],
+            device_id={"tm": dest},
+            device_id_type=MESH,
+        )
+
+    for d in range(NTM):
+
+        @pl.when(tm != d)
+        def _(d=d):
+            back_copy(d, tm).start()
+
+    back_in[tm] = back_out[...]
 
     adj = jnp.zeros((NBLK * ROWS, BLK), F32)
-    for q in (0, 1, 3, 2):
+    for q in range(4):
         for e in range(4 * q, 4 * q + 4):
-            if e:
-                from_back[e].wait_recv()
+
+            @pl.when(tm != e)
+            def _(e=e):
+                back_copy(e, e).wait_recv()
+
         adj += nn_dot(
             gt4[:, q * 4 * SLOTS : (q + 1) * 4 * SLOTS],
             back_in[4 * q : 4 * q + 4].reshape(4 * SLOTS, BLK),
@@ -404,20 +418,21 @@
     out_v[:, :HALF] += hop_in[2].astype(F32)
     near_left.wait_recv()
     out_v[:, HALF:] += hop_in[3].astype(F32)
-    outs = []
     for h, copy in enumerate((last_left, last_right)):
         cols = slice(h * HALF, (h + 1) * HALF)
         copy.wait_recv()
         out_v[:, cols] += hop_in[4 + h].astype(F32)
-        outs.append(load(out_v.at[:, cols], out_hbm.at[:, cols]))
     for copy in sends:
         copy.wait_send()
-    for copy in outs:
-        copy.wait()
-
-
-N_LOADS = 20
-N_SENDS = 3 + 3 + 6 + 8 + 15 + 7 + 15 + 8 + 6
+    for d in range(NTM):
+
+        @pl.when(tm != d)
+        def _(d=d):
+            back_copy(d, tm).wait_send()
+
+
+N_LOADS = 17
+N_SENDS = 3 + 3 + 6 + 8 + 15 + 7 + 8 + 6
 
 
 def local(
@@ -437,9 +452,9 @@
     i32 = jnp.int32
     return pl.pallas_call(
         kernel,
-        out_shape=jax.ShapeDtypeStruct((ROWS, COLS), F32),
+        out_shape=pltpu.VMEM((ROWS, COLS), F32),
         in_specs=[any_spec] * 10,
-        out_specs=any_spec,
+        out_specs=pl.BlockSpec(memory_space=pltpu.VMEM),
         scratch_shapes=[
             vm((ROWS, COLS), F32),
             vm((NX, 2, COLS, COLS), BF16),
@@ -452,7 +467,6 @@
             vm((1, 1), i32),
             vm((SLOTS, OBS), F32),
             vm((SLOTS, OBS), F32),
-            vm((ROWS, COLS), F32),
             vm((NX, 2, 2, ROWS, HALF), BF16),
             vm((ROWS, COLS), F32),
             vm((ROWS, TIMES), BF16),
@@ -479,6 +493,8 @@
             pltpu.SemaphoreType.DMA((N_LOADS,)),
             pltpu.SemaphoreType.DMA((N_SENDS,)),
             pltpu.SemaphoreType.DMA((N_SENDS,)),
+            pltpu.SemaphoreType.DMA((NTM,)),
+            pltpu.SemaphoreType.DMA((NTM,)),
         ],
         compiler_params=pltpu.CompilerParams(
             collective_id=0, has_side_effects=True, vmem_limit_bytes=56 * 1024 * 1024

time: 61.1 us -> 58.1 us (0.951)
  Pallas kernels: 58 us -> 56 us
  local copies, waits for them, and re-layouts: 1.89 us -> 0.8 us
    pallas_call x1, Pallas kernels: 58 us -> 56 us  [local(): pl.pallas_call(kernel, out_shape=pltpu.VMEM((ROWS, COLS), F32), in_specs=...]
    unnamed x1, local copies, waits for them, and re-layouts: 1.89 us -> 0.8 us
where the time goes in v3:
time: 58.1 us; the launch traced here: 57.5 us
  Pallas kernels  56 us (96%)
  local copies, waits for them, and re-layouts  0.8 us (1%)
  between operations  0.66 us (1%)
    pallas_call x1, Pallas kernels, local(): pl.pallas_call(kernel, out_shape=pltpu.VMEM((ROWS, COLS), F32), in_specs=...  56 us

profile of v3, /device:TPU:0, one launch (start us, length us, event | category | flops | bytes accessed | tf_op | source)
XLA Modules:
  0.0 57.5 jit_solution(11128417849537630163)
XLA Ops:
  0.7 56.0 %shard_map.100 = f32[128,1024]{1,0:T(8,128)S(1)} custom-call(f32[128,1024]{1,0:T(8,128)} %state_hbm.1, bf16[1024,8192]{1,0:T(8,128)(2,1)} %space_hbm.1, f32[2048,2048]{1,0:T(8,128)} %time_hbm.1, bf16[64,128,256]{2,1,0:T(8,128)(2,1)} %bitcast.4, s32[1,64]{1,0:T(1,128)} %bitcast.5, s32[1,64]{1,0:T(1,128)} %bitcast.6, s32[1,64]{1,0:T(1,128)} %bitcast.7, ...), custom_call_target="tpu_custom_call" | custom-call | tf_op jit(solution)/shard_map/pallas_call | solution.py:453
  56.7 0.8 %copy.12 = f32[128,1024]{1,0:T(8,128)} copy(f32[128,1024]{1,0:T(8,128)S(1)} %shard_map.100) | data formatting | bytes 1048576

commit v4 on v3

--- a/solution.py
+++ b/solution.py
@@ -49,6 +49,7 @@
     out_v,
     state_v,
     space_v,
+    space_t,
     time_v,
     foot_v,
     foot_t,
@@ -151,7 +152,7 @@
     load_space(OWN, 0)
     load_space(OWN, 1)
     ld_time = load(time_hbm.at[:, pl.ds(pl.multiple_of(tm * ROWS, ROWS), ROWS)], time_v)
-    for rel in (LEFT, RIGHT, OPP):
+    for rel in (OPP, LEFT, RIGHT):
         load_space(rel, 0)
         load_space(rel, 1)
     ld_foot = load(foot_hbm, foot_v)
@@ -211,6 +212,14 @@
         add_spread(OWN, 1, h)
     ld_time.wait()
     time_t[...] = time_v[...].T.astype(BF16)
+    for c in range(2):
+        ld_space[OPP, c].wait()
+
+        @pl.loop(0, COLS // BLK)
+        def _(n, c=c):
+            rows = pl.ds(pl.multiple_of(n * BLK, BLK), BLK)
+            space_t[c, :, rows] = space_v[OPP, c, rows, :].T
+
     got[LEFT, 0, 0].wait_recv()
     got[OPP, 0, 0] = block_to(LEFT, OPP, 0, right)
     got[RIGHT, 0, 1].wait_recv()
@@ -221,15 +230,10 @@
     for rel, h in ((LEFT, 0), (RIGHT, 1)):
         ld_space[rel, 0].wait()
         add_spread(rel, 0, h)
-    for rel, h in ((LEFT, 1), (RIGHT, 0)):
-        got[rel, 0, h].wait_recv()
-        got[rel, 1, h] = block_over(rel, h)
     for rel, h in ((LEFT, 0), (RIGHT, 1)):
         ld_space[rel, 1].wait()
         got[rel, 1, h].wait_recv()
         add_spread(rel, 1, h)
-    for rel, h in ((LEFT, 1), (RIGHT, 0)):
-        add_spread(rel, 0, h)
 
     for d in range(1, NX):
         from_z[d].wait_recv()
@@ -249,28 +253,36 @@
                 which_t == float(b), picked_t, 0.0
             ).astype(BF16)
 
+    for rel, h in ((LEFT, 1), (RIGHT, 0)):
+        got[rel, 0, h].wait_recv()
+        got[rel, 1, h] = block_over(rel, h)
+    for rel, h in ((LEFT, 1), (RIGHT, 0)):
+        add_spread(rel, 0, h)
+    for rel, h in ((LEFT, 1), (RIGHT, 0)):
+        got[rel, 1, h].wait_recv()
+        add_spread(rel, 1, h)
     for h in range(2):
         got[OPP, 0, h].wait_recv()
         got[OPP, 1, h] = block_over(OPP, h)
-    for rel, h in ((LEFT, 1), (RIGHT, 0)):
-        got[rel, 1, h].wait_recv()
-        add_spread(rel, 1, h)
     for c in range(2):
-        ld_space[OPP, c].wait()
         for h in range(2):
             if c:
                 got[OPP, 1, h].wait_recv()
-            add_spread(OPP, c, h)
+            spread_v[...] += nn_dot(xall[OPP, c, h], space_t[c, h * HALF : (h + 1) * HALF, :])
 
     spread4 = jnp.concatenate(
         [spread_v[:, b * BLK : (b + 1) * BLK].astype(BF16) for b in range(NBLK)], axis=0
     )
-    for m in range(NTM // 2):
-        part = nn_dot(g4[m * 2 * SLOTS : (m + 1) * 2 * SLOTS, :], spread4)
-        part_out[2 * m : 2 * m + 2] = part.astype(BF16).reshape(2, SLOTS, BLK)
     from_part = [None] * NTM
-    for e in FAR_FIRST:
-        from_part[e] = send(part_out.at[minus(e)], part_in.at[e], tm=minus(e))
+    for dz in (2, 1, 3, 0):
+        there = lax.rem(z + NX - dz, NX)
+        rows = pl.ds(pl.multiple_of(there * NX * SLOTS, NX * SLOTS), NX * SLOTS)
+        part = nn_dot(g4[rows, :], spread4)
+        part_out[pl.ds(there * NX, NX)] = part.astype(BF16).reshape(NX, SLOTS, BLK)
+        for dy in (2, 1, 3, 0):
+            e = dz * NX + dy
+            if e:
+                from_part[e] = send(part_out.at[minus(e)], part_in.at[e], tm=minus(e))
 
     for b in range(NBLK):
         for d in range(NX):
@@ -458,6 +470,7 @@
         scratch_shapes=[
             vm((ROWS, COLS), F32),
             vm((NX, 2, COLS, COLS), BF16),
+            vm((2, COLS, COLS), BF16),
             vm((TIMES, ROWS), F32),
             vm((SLOTS, OBS, BLK), BF16),
             vm((SLOTS, BLK, OBS), BF16),

time: 58.1 us -> 57.1 us (0.983)
  Pallas kernels: 56 us -> 55 us
    pallas_call x1, Pallas kernels: 56 us -> 55 us  [local(): pl.pallas_call(kernel, out_shape=pltpu.VMEM((ROWS, COLS), F32), in_specs=...]
where the time goes in v4:
time: 57.1 us; the launch traced here: 56.5 us
  Pallas kernels  55 us (96%)
  local copies, waits for them, and re-layouts  0.8 us (1%)
  between operations  0.66 us (1%)
    pallas_call x1, Pallas kernels, local(): pl.pallas_call(kernel, out_shape=pltpu.VMEM((ROWS, COLS), F32), in_specs=...  55 us

profile of v4, /device:TPU:0, one launch (start us, length us, event | category | flops | bytes accessed | tf_op | source)
XLA Modules:
  0.0 56.5 jit_solution(12475985269898890431)
XLA Ops:
  0.7 55.0 %shard_map.100 = f32[128,1024]{1,0:T(8,128)S(1)} custom-call(f32[128,1024]{1,0:T(8,128)} %state_hbm.1, bf16[1024,8192]{1,0:T(8,128)(2,1)} %space_hbm.1, f32[2048,2048]{1,0:T(8,128)} %time_hbm.1, bf16[64,128,256]{2,1,0:T(8,128)(2,1)} %bitcast.4, s32[1,64]{1,0:T(1,128)} %bitcast.5, s32[1,64]{1,0:T(1,128)} %bitcast.6, s32[1,64]{1,0:T(1,128)} %bitcast.7, ...), custom_call_target="tpu_custom_call" | custom-call | tf_op jit(solution)/shard_map/pallas_call | solution.py:465
  55.7 0.8 %copy.12 = f32[128,1024]{1,0:T(8,128)} copy(f32[128,1024]{1,0:T(8,128)S(1)} %shard_map.100) | data formatting | bytes 1048576

commit v5 on v4

--- a/solution.py
+++ b/solution.py
@@ -361,6 +361,9 @@
             back_copy(d, tm).start()
 
     back_in[tm] = back_out[...]
+    left_here = len(sends)
+    for copy in sends:
+        copy.wait_send()
 
     adj = jnp.zeros((NBLK * ROWS, BLK), F32)
     for q in range(4):
@@ -415,17 +418,25 @@
     own_terms(LEFT, 1)
     term_v[RIGHT, 0] = pair(RIGHT, 0)
     term_v[LEFT, 1] = pair(LEFT, 1)
+    to_sibling(OWN, 0)
+    to_sibling(OWN, 1)
+    for d in range(NTM):
+
+        @pl.when(tm != d)
+        def _(d=d):
+            back_copy(d, tm).wait_send()
+
     far_left.wait_recv()
     last_left = hop(4, term_v[RIGHT, 0] + hop_in[0].astype(F32), right)
     far_right.wait_recv()
     last_right = hop(5, term_v[LEFT, 1] + hop_in[1].astype(F32), left)
-    to_sibling(OWN, 0)
-    to_sibling(OWN, 1)
     own_terms(OWN, 0)
     own_terms(OWN, 1)
     for h in range(2):
         cols = slice(h * HALF, (h + 1) * HALF)
         out_v[:, cols] = state_v[:, cols] + pair(OWN, h)
+    for copy in sends[left_here:-2]:
+        copy.wait_send()
     near_right.wait_recv()
     out_v[:, :HALF] += hop_in[2].astype(F32)
     near_left.wait_recv()
@@ -434,13 +445,8 @@
         cols = slice(h * HALF, (h + 1) * HALF)
         copy.wait_recv()
         out_v[:, cols] += hop_in[4 + h].astype(F32)
-    for copy in sends:
+    for copy in sends[-2:]:
         copy.wait_send()
-    for d in range(NTM):
-
-        @pl.when(tm != d)
-        def _(d=d):
-            back_copy(d, tm).wait_send()
 
 
 N_LOADS = 17

time: 57.1 us -> 57 us (level)
  no operation moved by 1% of the time
where the time goes in v5:
time: 57 us; the launch traced here: 56.3 us
  Pallas kernels  54.9 us (96%)
  local copies, waits for them, and re-layouts  0.8 us (1%)
  between operations  0.66 us (1%)
    pallas_call x1, Pallas kernels, local(): pl.pallas_call(kernel, out_shape=pltpu.VMEM((ROWS, COLS), F32), in_specs=...  54.9 us

profile of v5, /device:TPU:0, one launch (start us, length us, event | category | flops | bytes accessed | tf_op | source)
XLA Modules:
  0.0 56.3 jit_solution(9351415124680143414)
XLA Ops:
  0.7 54.9 %shard_map.100 = f32[128,1024]{1,0:T(8,128)S(1)} custom-call(f32[128,1024]{1,0:T(8,128)} %state_hbm.1, bf16[1024,8192]{1,0:T(8,128)(2,1)} %space_hbm.1, f32[2048,2048]{1,0:T(8,128)} %time_hbm.1, bf16[64,128,256]{2,1,0:T(8,128)(2,1)} %bitcast.4, s32[1,64]{1,0:T(1,128)} %bitcast.5, s32[1,64]{1,0:T(1,128)} %bitcast.6, s32[1,64]{1,0:T(1,128)} %bitcast.7, ...), custom_call_target="tpu_custom_call" | custom-call | tf_op jit(solution)/shard_map/pallas_call | solution.py:471
  55.5 0.8 %copy.12 = f32[128,1024]{1,0:T(8,128)} copy(f32[128,1024]{1,0:T(8,128)S(1)} %shard_map.100) | data formatting | bytes 1048576

commit v6 on v5

--- a/solution.py
+++ b/solution.py
@@ -268,10 +268,14 @@
         for h in range(2):
             if c:
                 got[OPP, 1, h].wait_recv()
-            spread_v[...] += nn_dot(xall[OPP, c, h], space_t[c, h * HALF : (h + 1) * HALF, :])
+            spread = spread_v[...] + nn_dot(
+                xall[OPP, c, h], space_t[c, h * HALF : (h + 1) * HALF, :]
+            )
+            if not (c and h):
+                spread_v[...] = spread
 
     spread4 = jnp.concatenate(
-        [spread_v[:, b * BLK : (b + 1) * BLK].astype(BF16) for b in range(NBLK)], axis=0
+        [spread[:, b * BLK : (b + 1) * BLK].astype(BF16) for b in range(NBLK)], axis=0
     )
     from_part = [None] * NTM
     for dz in (2, 1, 3, 0):
@@ -405,9 +409,9 @@
     own_terms(OPP, 0)
     own_terms(OPP, 1)
     to_sibling(LEFT, 0)
-    to_sibling(RIGHT, 1)
     far_left = hop(0, pair(OPP, 0), right)
     far_right = hop(1, pair(OPP, 1), left)
+    to_sibling(RIGHT, 1)
     own_terms(LEFT, 0)
     own_terms(RIGHT, 1)
     near_right = hop(2, pair(LEFT, 0), left)

time: 57 us -> 57.2 us (level)
  no operation moved by 1% of the time
where the time goes in v6:
time: 57.2 us; the launch traced here: 56.3 us
  Pallas kernels  54.9 us (96%)
  local copies, waits for them, and re-layouts  0.8 us (1%)
  between operations  0.66 us (1%)
    pallas_call x1, Pallas kernels, local(): pl.pallas_call(kernel, out_shape=pltpu.VMEM((ROWS, COLS), F32), in_specs=...  54.9 us

profile of v6, /device:TPU:0, one launch (start us, length us, event | category | flops | bytes accessed | tf_op | source)
XLA Modules:
  0.0 56.3 jit_solution(15702370349605137743)
XLA Ops:
  0.7 54.9 %shard_map.100 = f32[128,1024]{1,0:T(8,128)S(1)} custom-call(f32[128,1024]{1,0:T(8,128)} %state_hbm.1, bf16[1024,8192]{1,0:T(8,128)(2,1)} %space_hbm.1, f32[2048,2048]{1,0:T(8,128)} %time_hbm.1, bf16[64,128,256]{2,1,0:T(8,128)(2,1)} %bitcast.4, s32[1,64]{1,0:T(1,128)} %bitcast.5, s32[1,64]{1,0:T(1,128)} %bitcast.6, s32[1,64]{1,0:T(1,128)} %bitcast.7, ...), custom_call_target="tpu_custom_call" | custom-call | tf_op jit(solution)/shard_map/pallas_call | solution.py:475
  55.5 0.8 %copy.12 = f32[128,1024]{1,0:T(8,128)} copy(f32[128,1024]{1,0:T(8,128)S(1)} %shard_map.100) | data formatting | bytes 1048576
